TPU v7x, 32 devices: a whole 2x2x4 slice. The times are simulated.
32 devices in a mesh: row: 4 (over y, x), col: 8 (over z, core).
Axes of the slice: x: 2, y: 2, z: 4, core: 2. Of those that a mesh axis runs over, the one named last changes fastest.
Arguments:
- features: float32 [16384, 256], P(('col', 'row')), may hold values from -6 to 6
- weight: float32 [256, 256], replicated, may hold values from -0.375 to 0.375
- cotangent: float32 [16384, 256], P(('row', 'col')), may hold values from -6 to 6
- tile_values: float32 [4, 8, 128, 128, 128], P('row', 'col'), as said below
- tile_rows: int32 [4, 8, 128], P('row', 'col'), may hold values from 0 to 31
- tile_cols: int32 [4, 8, 128], P('row', 'col'), may hold values from 0 to 15
- tile_count: int32 [4, 8], P('row', 'col'), may hold values from 16 to 128, as said below
Outputs:
- output: float32 [16384, 256], P(('row', 'col'))
- feature_grad: float32 [16384, 256], P(('col', 'row'))
- weight_grad: float32 [256, 256], replicated
Inputs may be any that keep to these rules, and one draw needn't show every extreme that they name: `tile_count`: the number of live slots of a grid cell is 128, 64, 32 or 16; some cell has 128. `tile_values`: entries are zero or positive.
All inputs are finite; a program needn't handle non-finite values.
Results may differ from a plain program's by a relative error of at most 0.0001.
Values sent between devices are 32-bit elements; how exact they have to be, the bound alone decides.
A program may use at most 128 MiB of HBM per device.

v0:
```python
import functools
import math

import jax
import jax.numpy as jnp
from jax import lax
from jax.experimental import pallas as pl
from jax.experimental.pallas import tpu as pltpu
from jax.sharding import PartitionSpec as P

F32 = jnp.float32
BF16 = jnp.bfloat16
MESH = pl.DeviceIdType.MESH
VMEM_LIMIT = 60 * 1024 * 1024
HIGHEST = lax.Precision.HIGHEST


def split(x):
    hi = x.astype(BF16)
    return hi, (x - hi.astype(F32)).astype(BF16)


def params(collective_id=None):
    if collective_id is None:
        return pltpu.CompilerParams(vmem_limit_bytes=VMEM_LIMIT)
    return pltpu.CompilerParams(
        vmem_limit_bytes=VMEM_LIMIT, collective_id=collective_id, has_side_effects=True
    )


def tile_kernel(group, transpose, fetch_ref, put_ref, count_ref, tiles_ref, source_ref, out_ref, hi_ref, lo_ref):
    step = pl.program_id(0)
    edge = tiles_ref.shape[1]

    @pl.when(step == 0)
    def _():
        out_ref[...] = jnp.zeros_like(out_ref)

        @pl.loop(0, source_ref.shape[0] // edge)
        def _(b):
            rows = pl.ds(pl.multiple_of(b * edge, edge), edge)
            hi, lo = split(source_ref[rows, :])
            hi_ref[rows, :] = hi
            lo_ref[rows, :] = lo

    @pl.when(step * group < count_ref[0])
    def _():
        for t in range(group):
            slot = step * group + t
            fetch = pl.ds(pl.multiple_of(fetch_ref[slot] * edge, edge), edge)
            put = pl.ds(pl.multiple_of(put_ref[slot] * edge, edge), edge)
            tile = tiles_ref[t]
            if transpose:
                tile = tile.T
            a_hi, a_lo = split(tile)
            b_hi, b_lo = hi_ref[fetch, :], lo_ref[fetch, :]
            product = jnp.dot(
                jnp.concatenate([a_hi, a_lo], axis=1),
                jnp.concatenate([b_hi, b_hi], axis=0),
                preferred_element_type=F32,
            ) + jnp.dot(a_hi, b_lo, preferred_element_type=F32)
            out_ref[put, :] += product


def combine_tiles(tiles, fetch_ids, put_ids, count, source, out_rows, transpose):
    slots, edge, _ = tiles.shape
    width = source.shape[1]
    group = math.gcd(16, slots)

    def tile_index(i, fetch, put, n):
        return (jnp.minimum(i, (n[0] - 1) // group), 0, 0)

    return pl.pallas_call(
        functools.partial(tile_kernel, group, transpose),
        grid_spec=pltpu.PrefetchScalarGridSpec(
            num_scalar_prefetch=3,
            grid=(slots // group,),
            in_specs=[
                pl.BlockSpec((group, edge, edge), tile_index),
                pl.BlockSpec(source.shape, lambda i, *_: (0, 0), pipeline_mode=pl.Buffered(1)),
            ],
            out_specs=pl.BlockSpec((out_rows, width), lambda i, *_: (0, 0), pipeline_mode=pl.Buffered(1)),
            scratch_shapes=[pltpu.VMEM(source.shape, BF16), pltpu.VMEM(source.shape, BF16)],
        ),
        out_shape=jax.ShapeDtypeStruct((out_rows, width), F32),
        compiler_params=params(),
    )(fetch_ids, put_ids, count, tiles, source)


def gather_kernel(n, x_ref, out_ref, send_sem, recv_sem, own_sem):
    me = lax.axis_index("row")
    rows = x_ref.shape[0]
    barrier = pltpu.get_barrier_semaphore()
    for j in range(1, n):
        pl.semaphore_signal(barrier, inc=1, device_id={"row": lax.rem(me + j, n)}, device_id_type=MESH)
    pl.semaphore_wait(barrier, n - 1)

    def copy(j, block):
        return pltpu.make_async_remote_copy(
            src_ref=x_ref,
            dst_ref=out_ref.at[pl.ds(pl.multiple_of(block * rows, rows), rows), :],
            send_sem=send_sem.at[j],
            recv_sem=recv_sem.at[j],
            device_id={"row": lax.rem(me + j, n)},
            device_id_type=MESH,
        )

    for j in range(1, n):
        copy(j, me).start()
    own = pltpu.make_async_copy(x_ref, out_ref.at[pl.ds(pl.multiple_of(me * rows, rows), rows), :], own_sem)
    own.start()
    own.wait()
    for j in range(1, n):
        copy(j, me).wait_send()
        copy(j, lax.rem(me + n - j, n)).wait_recv()


def gather_rows(x, n):
    return pl.pallas_call(
        functools.partial(gather_kernel, n),
        in_specs=[pl.BlockSpec(memory_space=pl.ANY)],
        out_specs=pl.BlockSpec(memory_space=pl.ANY),
        out_shape=jax.ShapeDtypeStruct((n * x.shape[0], x.shape[1]), F32),
        scratch_shapes=[
            pltpu.SemaphoreType.DMA((n,)),
            pltpu.SemaphoreType.DMA((n,)),
            pltpu.SemaphoreType.DMA,
        ],
        compiler_params=params(0),
    )(x)


def middle_kernel(
    zs, chunks,
    part_ref, weight_ref, cot_ref,
    out_ref, grads_ref, term_ref,
    acc, mate, from_left, from_right, grad,
    own_sem, mate_send, mate_recv, right_send, right_recv, left_send, left_recv,
    on_send, back_send, line_recv, share_send, share_recv, keep_sem,
):
    col = lax.axis_index("col")
    z, k = lax.div(col, 2), lax.rem(col, 2)
    rows = cot_ref.shape[0]
    size = rows // chunks
    pair = {"col": z * 2 + (1 - k)}
    right, left = {"col": jnp.minimum(z + 1, zs - 1) * 2 + k}, {"col": jnp.maximum(z - 1, 0) * 2 + k}
    has_left, has_right = z > 0, z < zs - 1

    barrier = pltpu.get_barrier_semaphore()
    pl.semaphore_signal(barrier, inc=1, device_id=pair, device_id_type=MESH)

    @pl.when(has_left)
    def _():
        pl.semaphore_signal(barrier, inc=1, device_id=left, device_id_type=MESH)

    @pl.when(has_right)
    def _():
        pl.semaphore_signal(barrier, inc=1, device_id=right, device_id_type=MESH)

    pl.semaphore_wait(barrier, 1 + has_left.astype(jnp.int32) + has_right.astype(jnp.int32))

    def span(c):
        return pl.ds(pl.multiple_of(c * size, size), size)

    def place(owner, core, c):
        return pl.ds(pl.multiple_of((owner * 2 + core) * rows + c * size, size), size)

    def remote(src, dst, send, recv, device):
        return pltpu.make_async_remote_copy(
            src_ref=src, dst_ref=dst, send_sem=send, recv_sem=recv, device_id=device, device_id_type=MESH
        )

    def own_copy(d):
        block = part_ref.at[pl.ds(pl.multiple_of((d * 2 + k) * rows, rows), rows), :]
        return pltpu.make_async_copy(block, acc.at[d], own_sem.at[d])

    def mate_copy(d, c):
        return remote(
            part_ref.at[place(d, 1 - k, c), :], mate.at[d, span(c)], mate_send.at[d, c], mate_recv.at[d, c], pair
        )

    def to_right(d, c):
        return remote(acc.at[d, span(c)], from_left.at[d, span(c)], right_send.at[d, c], right_recv.at[d, c], right)

    def to_left(d, c):
        return remote(acc.at[d, span(c)], from_right.at[d, span(c)], left_send.at[d, c], left_recv.at[d, c], left)

    def own_on(c):
        return remote(grad.at[span(c)], grads_ref.at[place(z, k, c), :], on_send.at[z, c], line_recv.at[z, c], right)

    def own_back(c):
        return remote(grad.at[span(c)], grads_ref.at[place(z, k, c), :], back_send.at[c], line_recv.at[z, c], left)

    def own_share(c):
        return remote(grad.at[span(c)], grads_ref.at[place(z, k, c), :], share_send.at[z, c], share_recv.at[z, c], pair)

    def own_keep(c):
        return pltpu.make_async_copy(grad.at[span(c)], grads_ref.at[place(z, k, c), :], keep_sem.at[c])

    def pass_on(s, c, device):
        where = grads_ref.at[place(s, k, c), :]
        return remote(where, where, on_send.at[s, c], line_recv.at[s, c], device)

    def share(s, core, c):
        where = grads_ref.at[place(s, core, c), :]
        return remote(where, where, share_send.at[s, c], share_recv.at[s, c], pair)

    @pl.loop(0, zs)
    def _(d):
        own_copy(d).start()

    @pl.loop(0, chunks)
    def _(c):
        @pl.loop(0, zs)
        def _(d):
            mate_copy(d, c).start()

    @pl.loop(0, zs)
    def _(d):
        own_copy(d).wait()

    def add_mate(d, c):
        mate_copy(d, c).wait_recv()
        acc[d, span(c)] += mate[d, span(c)]

    def reduce_chunk(c):
        @pl.loop(0, zs - 1)
        def _(i):
            far = zs - 1 - i

            @pl.when(far > z)
            def _():
                add_mate(far, c)

                @pl.when(has_left)
                def _():
                    to_right(far, c).wait_recv()
                    acc[far, span(c)] += from_left[far, span(c)]

                to_right(far, c).start()

            @pl.when(i < z)
            def _():
                add_mate(i, c)

                @pl.when(has_right)
                def _():
                    to_left(i, c).wait_recv()
                    acc[i, span(c)] += from_right[i, span(c)]

                to_left(i, c).start()

    def finish_chunk(c):
        add_mate(z, c)

        @pl.when(has_left)
        def _():
            to_right(z, c).wait_recv()
            acc[z, span(c)] += from_left[z, span(c)]

        @pl.when(has_right)
        def _():
            to_left(z, c).wait_recv()
            acc[z, span(c)] += from_right[z, span(c)]

        summed = acc[z, span(c)]
        weight = weight_ref[...]
        pre = jnp.dot(summed, weight, precision=HIGHEST, preferred_element_type=F32)
        sigma = jax.nn.sigmoid(pre)
        out_ref[span(c), :] = pre * sigma
        grad_pre = cot_ref[span(c), :] * sigma * (1.0 + pre * (1.0 - sigma))
        grad[span(c)] = lax.dot_general(
            grad_pre, weight, (((1,), (1,)), ((), ())), precision=HIGHEST, preferred_element_type=F32
        )

        @pl.when(has_right)
        def _():
            own_on(c).start()

        @pl.when(has_left)
        def _():
            own_back(c).start()

        own_share(c).start()
        own_keep(c).start()
        term_ref[...] += lax.dot_general(
            summed, grad_pre, (((0,), (0,)), ((), ())), precision=HIGHEST, preferred_element_type=F32
        )

    def relay_chunk(c):
        @pl.loop(1, zs)
        def _(i):
            low, high = z - i, z + i

            @pl.when(low >= 0)
            def _():
                pass_on(low, c, right).wait_recv()

                @pl.when(has_right)
                def _():
                    pass_on(low, c, right).start()

                share(low, k, c).start()

            @pl.when(high < zs)
            def _():
                pass_on(high, c, left).wait_recv()

                @pl.when(has_left)
                def _():
                    pass_on(high, c, left).start()

                share(high, k, c).start()

    term_ref[...] = jnp.zeros_like(term_ref)

    @pl.loop(0, chunks + 2)
    def _(s):
        @pl.when(s < chunks)
        def _():
            reduce_chunk(s)

        @pl.when((s >= 1) & (s <= chunks))
        def _():
            finish_chunk(s - 1)

        @pl.when(s >= 2)
        def _():
            relay_chunk(s - 2)

    @pl.loop(0, chunks)
    def _(c):
        own_share(c).wait_send()
        own_keep(c).wait()

        @pl.when(has_right)
        def _():
            own_on(c).wait_send()

        @pl.when(has_left)
        def _():
            own_back(c).wait_send()

        @pl.loop(0, zs)
        def _(d):
            mate_copy(d, c).wait_send()
            share(d, 1 - k, c).wait_recv()

            @pl.when(d > z)
            def _():
                to_right(d, c).wait_send()
                share(d, k, c).wait_send()

                @pl.when(has_left)
                def _():
                    pass_on(d, c, left).wait_send()

            @pl.when(d < z)
            def _():
                to_left(d, c).wait_send()
                share(d, k, c).wait_send()

                @pl.when(has_right)
                def _():
                    pass_on(d, c, right).wait_send()


def middle(part, weight, cotangent, n_col):
    rows, width = cotangent.shape
    zs, chunks = n_col // 2, 4
    grid2 = pltpu.SemaphoreType.DMA((zs, chunks))
    vmem = pl.BlockSpec(memory_space=pltpu.VMEM)
    blocks = pltpu.VMEM((zs, rows, width), F32)
    return pl.pallas_call(
        functools.partial(middle_kernel, zs, chunks),
        in_specs=[pl.BlockSpec(memory_space=pl.ANY), vmem, vmem],
        out_specs=(vmem, pl.BlockSpec(memory_space=pl.ANY), vmem),
        out_shape=(
            jax.ShapeDtypeStruct((rows, width), F32),
            jax.ShapeDtypeStruct((n_col * rows, width), F32),
            jax.ShapeDtypeStruct((width, width), F32),
        ),
        scratch_shapes=[
            blocks, blocks, blocks, blocks, pltpu.VMEM((rows, width), F32),
            pltpu.SemaphoreType.DMA((zs,)), grid2, grid2, grid2, grid2, grid2, grid2,
            grid2, pltpu.SemaphoreType.DMA((chunks,)), grid2, grid2, grid2, pltpu.SemaphoreType.DMA((chunks,)),
        ],
        compiler_params=params(1),
    )(part, weight, cotangent)


def last_kernel(
    n_row, n_col, scale,
    part_ref, term_ref,
    out_ref, total_ref,
    arrived, first, second,
    own_sem, send_sem, recv_sem, send1, recv1, send2, recv2, send3, recv3,
):
    row, col = lax.axis_index("row"), lax.axis_index("col")
    rows = out_ref.shape[0]
    piece = term_ref.shape[0] // n_col
    barrier = pltpu.get_barrier_semaphore()
    for j in range(1, n_row):
        pl.semaphore_signal(barrier, inc=1, device_id={"row": lax.rem(row + j, n_row)}, device_id_type=MESH)
    for j in range(1, n_col):
        pl.semaphore_signal(barrier, inc=1, device_id={"col": lax.rem(col + j, n_col)}, device_id_type=MESH)
    pl.semaphore_wait(barrier, n_row + n_col - 2)

    def block(i):
        return part_ref.at[pl.ds(pl.multiple_of(i * rows, rows), rows), :]

    def rows_of(i):
        return pl.ds(pl.multiple_of(i * piece, piece), piece)

    def bulk(j):
        to = lax.rem(row + j, n_row)
        return pltpu.make_async_remote_copy(
            src_ref=block(to), dst_ref=arrived.at[j], send_sem=send_sem.at[j], recv_sem=recv_sem.at[j],
            device_id={"row": to}, device_id_type=MESH,
        )

    def scatter(j):
        to = lax.rem(col + j, n_col)
        return pltpu.make_async_remote_copy(
            src_ref=term_ref.at[rows_of(to), :], dst_ref=first.at[j], send_sem=send1.at[j], recv_sem=recv1.at[j],
            device_id={"col": to}, device_id_type=MESH,
        )

    def exchange(j, slot):
        return pltpu.make_async_remote_copy(
            src_ref=first.at[0], dst_ref=second.at[slot], send_sem=send2.at[j], recv_sem=recv2.at[j],
            device_id={"row": lax.rem(row + j, n_row)}, device_id_type=MESH,
        )

    def spread(j, owner):
        where = total_ref.at[rows_of(owner), :]
        return pltpu.make_async_remote_copy(
            src_ref=where, dst_ref=where, send_sem=send3.at[j], recv_sem=recv3.at[j],
            device_id={"col": lax.rem(col + j, n_col)}, device_id_type=MESH,
        )

    own = pltpu.make_async_copy(block(row), arrived.at[0], own_sem)
    own.start()
    for j in range(1, n_col):
        scatter(j).start()
    bulk(1).start()
    first[0] = term_ref[rows_of(col), :]
    for j in range(1, n_col):
        scatter(j).wait_recv()
        first[0] += first[j]
    for j in range(1, n_row):
        exchange(j, row).start()
    for j in range(2, n_row):
        bulk(j).start()
    second[row] = first[0]
    for j in range(1, n_row):
        exchange(j, lax.rem(row + n_row - j, n_row)).wait_recv()
    summed = second[0]
    for i in range(1, n_row):
        summed += second[i]
    total_ref[rows_of(col), :] = summed * scale
    for j in range(1, n_col):
        spread(j, col).start()
    own.wait()
    for j in range(1, n_row):
        bulk(j).wait_recv()
    out_ref[...] = arrived[0]
    for j in range(1, n_row):
        out_ref[...] += arrived[j]
    for j in range(1, n_row):
        bulk(j).wait_send()
        exchange(j, row).wait_send()
    for j in range(1, n_col):
        scatter(j).wait_send()
        spread(j, col).wait_send()
        spread(j, lax.rem(col + n_col - j, n_col)).wait_recv()


def last(part, term, n_row, n_col, scale):
    rows, width = part.shape[0] // n_row, part.shape[1]
    piece = term.shape[0] // n_col
    vmem = pl.BlockSpec(memory_space=pltpu.VMEM)
    by_row, by_col = pltpu.SemaphoreType.DMA((n_row,)), pltpu.SemaphoreType.DMA((n_col,))
    return pl.pallas_call(
        functools.partial(last_kernel, n_row, n_col, scale),
        in_specs=[pl.BlockSpec(memory_space=pl.ANY), vmem],
        out_specs=(vmem, vmem),
        out_shape=(jax.ShapeDtypeStruct((rows, width), F32), jax.ShapeDtypeStruct(term.shape, F32)),
        scratch_shapes=[
            pltpu.VMEM((n_row, rows, width), F32),
            pltpu.VMEM((n_col, piece, width), F32),
            pltpu.VMEM((n_row, piece, width), F32),
            pltpu.SemaphoreType.DMA, by_row, by_row, by_col, by_col, by_row, by_row, by_col, by_col,
        ],
        compiler_params=params(2),
    )(part, term)


def local(n_row, n_col, features, weight, cotangent, tile_values, tile_rows, tile_cols, tile_count):
    tiles, row_ids, col_ids = tile_values[0, 0], tile_rows[0, 0], tile_cols[0, 0]
    count = tile_count.reshape(1)
    rows = features.shape[0]
    gathered = gather_rows(features, n_row)
    part = combine_tiles(tiles, col_ids, row_ids, count, gathered, rows * n_col, False)
    output, grads, term = middle(part, weight, cotangent, n_col)
    part_grad = combine_tiles(tiles, row_ids, col_ids, count, grads, rows * n_row, True)
    scale = 1.0 / math.sqrt(rows * n_row * n_col)
    returned, weight_grad = last(part_grad, term, n_row, n_col, scale)
    return (output, returned, weight_grad)


def solution(mesh):
    placed = (
        P(("col", "row"), None),
        P(),
        P(("row", "col"), None),
        P("row", "col", None, None, None),
        P("row", "col", None),
        P("row", "col", None),
        P("row", "col"),
    )
    return jax.shard_map(
        functools.partial(local, mesh.shape["row"], mesh.shape["col"]),
        mesh=mesh,
        in_specs=placed,
        out_specs=(P(("row", "col"), None), P(("col", "row"), None), P()),
        check_vma=False,
    )
```

profile of v0, /device:TPU:0, one launch (start us, length us, event | category | flops | bytes accessed | tf_op | source)
XLA Modules:
  0.0 182.5 jit_solution(15882605680225299259)
XLA Ops:
  1.3 27.8 %shard_map.94.source_ref = f32[2048,256]{1,0:T(8,128)} custom-call(f32[512,256]{1,0:T(8,128)} %x_ref.1), custom_call_target="tpu_custom_call" | custom-call | tf_op jit(solution)/shard_map/pallas_call | solution.py:119
  29.1 6.8 %shard_map.95.part_ref = f32[4096,256]{1,0:T(8,128)} custom-call(s32[128]{0:T(128)} %bitcast.8, s32[128]{0:T(128)} %bitcast.10, s32[1]{0:T(128)} %bitcast.4.count_ref, f32[128,128,128]{2,1,0:T(8,128)} %bitcast.6, f32[2048,256]{1,0:T(8,128)} %shard_map.94.source_ref), custom_call_target="tpu_custom_call" | custom-call | tf_op jit(solution)/shard_map/pallas_call | solution.py:73
  35.9 92.3 %shard_map.96 = (f32[512,256]{1,0:T(8,128)}, f32[4096,256]{1,0:T(8,128)}, f32[256,256]{1,0:T(8,128)}) custom-call(f32[4096,256]{1,0:T(8,128)} %shard_map.95.part_ref, f32[256,256]{1,0:T(8,128)} %weight_ref.1, f32[512,256]{1,0:T(8,128)} %cot_ref.1), custom_call_target="tpu_custom_call" | custom-call | tf_op jit(solution)/shard_map/pallas_call | solution.py:374
  128.2 0.0 copy-start
  128.2 7.3 %shard_map.97.part_ref = f32[2048,256]{1,0:T(8,128)} custom-call(s32[128]{0:T(128)} %bitcast.11, s32[128]{0:T(128)} %bitcast.9, s32[1]{0:T(128)} %bitcast.5.count_ref, f32[128,128,128]{2,1,0:T(8,128)} %bitcast.7, f32[4096,256]{1,0:T(8,128)} %get-tuple-element.9.source_ref), custom_call_target="tpu_custom_call" | custom-call | tf_op jit(solution)/shard_map/pallas_call | solution.py:73
  135.5 42.7 %shard_map.98 = (f32[512,256]{1,0:T(8,128)}, f32[256,256]{1,0:T(8,128)}) custom-call(f32[2048,256]{1,0:T(8,128)} %shard_map.97.part_ref, f32[256,256]{1,0:T(8,128)} %get-tuple-element.10.term_ref), custom_call_target="tpu_custom_call" | custom-call | tf_op jit(solution)/shard_map/pallas_call | solution.py:484
  178.2 0.0 copy-done
  178.2 0.8 copy.14
  179.0 1.9 %copy.15 = f32[512,256]{1,0:T(8,128)} copy(f32[512,256]{1,0:T(8,128)} %get-tuple-element.17) | data formatting | bytes 1048576
  180.8 1.7 copy.16
Async XLA Ops:
  128.2 50.0 %copy-start = (f32[512,256]{1,0:T(8,128)S(1)}, f32[512,256]{1,0:T(8,128)}, u32[]{:S(2)}) copy-start(f32[512,256]{1,0:T(8,128)} %get-tuple-element.16) | copy-start | bytes 1572868
where the time goes:
time: 185 us; the launch traced here: 183 us
  Pallas kernels  177 us (96%)
  local copies, waits for them, and re-layouts  4.34 us (2%)
    pallas_call x1, Pallas kernels, middle(): pl.pallas_call(functools.partial(middle_kernel, zs, chunks), in_specs=[pl...  92.3 us
    pallas_call x1, Pallas kernels, last(): pl.pallas_call(functools.partial(last_kernel, n_row, n_col, scale), in_sp...  42.7 us
    pallas_call x1, Pallas kernels, gather_rows(): pl.pallas_call(functools.partial(gather_kernel, n), in_specs=[pl.BlockSpe...  27.8 us
    pallas_call x2, Pallas kernels, combine_tiles(): pl.pallas_call(functools.partial(tile_kernel, group, transpose), grid_spe...  14.1 us
    unnamed x5, local copies, waits for them, and re-layouts  4.34 us

commit v1 on v0

--- a/solution.py
+++ b/solution.py
@@ -12,12 +12,19 @@
 BF16 = jnp.bfloat16
 MESH = pl.DeviceIdType.MESH
 VMEM_LIMIT = 60 * 1024 * 1024
+DENSE = True
 HIGHEST = lax.Precision.HIGHEST
 
 
 def split(x):
     hi = x.astype(BF16)
     return hi, (x - hi.astype(F32)).astype(BF16)
+
+
+def dot3(a, b_hi, b_lo):
+    a_hi, a_lo = split(a)
+    dot = functools.partial(jnp.dot, preferred_element_type=F32)
+    return dot(a_hi, b_hi) + (dot(a_lo, b_hi) + dot(a_hi, b_lo))
 
 
 def params(collective_id=None):
@@ -115,15 +122,74 @@
         copy(j, lax.rem(me + n - j, n)).wait_recv()
 
 
-def gather_rows(x, n):
+def gather_square_kernel(parts, x_ref, out_ref, send_sem, recv_sem, own_sem):
+    me = lax.axis_index("row")
+    rows = x_ref.shape[0]
+    size = rows // parts
+    x_bit, y_bit = lax.rem(me, 2), lax.div(me, 2)
+    by_x, by_y = y_bit * 2 + (1 - x_bit), (1 - y_bit) * 2 + x_bit
+    corner = 3 - me
+    barrier = pltpu.get_barrier_semaphore()
+    for peer in (by_x, by_y):
+        pl.semaphore_signal(barrier, inc=1, device_id={"row": peer}, device_id_type=MESH)
+    pl.semaphore_wait(barrier, 2)
+
+    def at(owner, q):
+        return out_ref.at[pl.ds(pl.multiple_of(owner * rows + q * size, size), size), :]
+
+    def copy(source, owner, q, kind, peer):
+        return pltpu.make_async_remote_copy(
+            src_ref=source, dst_ref=at(owner, q), send_sem=send_sem.at[kind, q], recv_sem=recv_sem.at[kind, q],
+            device_id={"row": peer}, device_id_type=MESH,
+        )
+
+    def own(q, kind):
+        return copy(x_ref.at[pl.ds(q * size, size), :], me, q, kind, (by_x, by_y)[kind])
+
+    half = parts // 2
+    order = list(range(parts))
+    for a, b in zip(order, order[half:] + order[:half]):
+        own(a, 0).start()
+        own(b, 1).start()
+    keep = pltpu.make_async_copy(x_ref, out_ref.at[pl.ds(pl.multiple_of(me * rows, rows), rows), :], own_sem)
+    keep.start()
+
+    def arrival(owner, q, kind):
+        return copy(at(owner, q), owner, q, kind, (by_x, by_y)[kind % 2])
+
+    def onward(q):
+        if q < half:
+            return copy(at(by_x, q), by_x, q, 2, by_y)
+        return copy(at(by_y, q), by_y, q, 2, by_x)
+
+    for q in range(half):
+        arrival(by_x, q, 0).wait_recv()
+        onward(q).start()
+        arrival(by_y, q + half, 1).wait_recv()
+        onward(q + half).start()
+    keep.wait()
+    for q in range(parts):
+        if q >= half:
+            arrival(by_x, q, 0).wait_recv()
+        else:
+            arrival(by_y, q, 1).wait_recv()
+        arrival(corner, q, 2).wait_recv()
+        own(q, 0).wait_send()
+        own(q, 1).wait_send()
+        onward(q).wait_send()
+
+
+def gather_rows(x, n, parts=8):
+    square = n == 4
+    shape = (3, parts) if square else (n,)
     return pl.pallas_call(
-        functools.partial(gather_kernel, n),
+        functools.partial(gather_square_kernel, parts) if square else functools.partial(gather_kernel, n),
         in_specs=[pl.BlockSpec(memory_space=pl.ANY)],
         out_specs=pl.BlockSpec(memory_space=pl.ANY),
         out_shape=jax.ShapeDtypeStruct((n * x.shape[0], x.shape[1]), F32),
         scratch_shapes=[
-            pltpu.SemaphoreType.DMA((n,)),
-            pltpu.SemaphoreType.DMA((n,)),
+            pltpu.SemaphoreType.DMA(shape),
+            pltpu.SemaphoreType.DMA(shape),
             pltpu.SemaphoreType.DMA,
         ],
         compiler_params=params(0),
@@ -131,10 +197,10 @@
 
 
 def middle_kernel(
-    zs, chunks,
+    zs, chunks, skew, extra, hop,
     part_ref, weight_ref, cot_ref,
     out_ref, grads_ref, term_ref,
-    acc, mate, from_left, from_right, grad,
+    acc, mate, from_left, from_right, grad, inner, w_hi, w_lo, t_hi, t_lo,
     own_sem, mate_send, mate_recv, right_send, right_recv, left_send, left_recv,
     on_send, back_send, line_recv, share_send, share_recv, keep_sem,
 ):
@@ -223,32 +289,30 @@
         mate_copy(d, c).wait_recv()
         acc[d, span(c)] += mate[d, span(c)]
 
-    def reduce_chunk(c):
-        @pl.loop(0, zs - 1)
+    def reduce_right(c):
+        @pl.loop(0, zs - 1 - z)
         def _(i):
             far = zs - 1 - i
-
-            @pl.when(far > z)
+            add_mate(far, c)
+
+            @pl.when(has_left)
             def _():
-                add_mate(far, c)
-
-                @pl.when(has_left)
-                def _():
-                    to_right(far, c).wait_recv()
-                    acc[far, span(c)] += from_left[far, span(c)]
-
-                to_right(far, c).start()
-
-            @pl.when(i < z)
+                to_right(far, c).wait_recv()
+                acc[far, span(c)] += from_left[far, span(c)]
+
+            to_right(far, c).start()
+
+    def reduce_left(c):
+        @pl.loop(0, z)
+        def _(i):
+            add_mate(i, c)
+
+            @pl.when(has_right)
             def _():
-                add_mate(i, c)
-
-                @pl.when(has_right)
-                def _():
-                    to_left(i, c).wait_recv()
-                    acc[i, span(c)] += from_right[i, span(c)]
-
-                to_left(i, c).start()
+                to_left(i, c).wait_recv()
+                acc[i, span(c)] += from_right[i, span(c)]
+
+            to_left(i, c).start()
 
     def finish_chunk(c):
         add_mate(z, c)
@@ -263,15 +327,14 @@
             to_left(z, c).wait_recv()
             acc[z, span(c)] += from_right[z, span(c)]
 
-        summed = acc[z, span(c)]
-        weight = weight_ref[...]
-        pre = jnp.dot(summed, weight, precision=HIGHEST, preferred_element_type=F32)
-        sigma = jax.nn.sigmoid(pre)
-        out_ref[span(c), :] = pre * sigma
-        grad_pre = cot_ref[span(c), :] * sigma * (1.0 + pre * (1.0 - sigma))
-        grad[span(c)] = lax.dot_general(
-            grad_pre, weight, (((1,), (1,)), ((), ())), precision=HIGHEST, preferred_element_type=F32
-        )
+        if DENSE:
+            summed = acc[z, span(c)]
+            pre = dot3(summed, w_hi[...], w_lo[...])
+            sigma = jax.nn.sigmoid(pre)
+            out_ref[span(c), :] = pre * sigma
+            grad_pre = cot_ref[span(c), :] * sigma * (1.0 + pre * (1.0 - sigma))
+            inner[span(c), :] = grad_pre
+            grad[span(c)] = dot3(grad_pre, t_hi[...], t_lo[...])
 
         @pl.when(has_right)
         def _():
@@ -283,50 +346,48 @@
 
         own_share(c).start()
         own_keep(c).start()
-        term_ref[...] += lax.dot_general(
-            summed, grad_pre, (((0,), (0,)), ((), ())), precision=HIGHEST, preferred_element_type=F32
-        )
-
-    def relay_chunk(c):
+
+    def relay(source, c, has_next, device):
+        pass_on(source, c, device).wait_recv()
+
+        @pl.when(has_next)
+        def _():
+            pass_on(source, c, device).start()
+
+        share(source, k, c).start()
+
+    w_hi[...], w_lo[...] = split(weight_ref[...])
+    t_hi[...], t_lo[...] = split(weight_ref[...].T)
+
+    def sent(owner):
+        return skew * jnp.maximum(owner, zs - 1 - owner) + extra
+
+    def at_step(c, act):
+        @pl.when((c >= 0) & (c < chunks))
+        def _():
+            act(c)
+
+    @pl.loop(0, chunks + (skew + hop) * (zs - 1) + extra)
+    def _(s):
+        at_step(s - skew * z, reduce_right)
+        at_step(s - skew * (zs - 1 - z), reduce_left)
+        at_step(s - sent(z), finish_chunk)
+
         @pl.loop(1, zs)
         def _(i):
             low, high = z - i, z + i
 
             @pl.when(low >= 0)
             def _():
-                pass_on(low, c, right).wait_recv()
-
-                @pl.when(has_right)
-                def _():
-                    pass_on(low, c, right).start()
-
-                share(low, k, c).start()
+                at_step(s - sent(low) - hop * i, lambda c: relay(low, c, has_right, right))
 
             @pl.when(high < zs)
             def _():
-                pass_on(high, c, left).wait_recv()
-
-                @pl.when(has_left)
-                def _():
-                    pass_on(high, c, left).start()
-
-                share(high, k, c).start()
-
-    term_ref[...] = jnp.zeros_like(term_ref)
-
-    @pl.loop(0, chunks + 2)
-    def _(s):
-        @pl.when(s < chunks)
-        def _():
-            reduce_chunk(s)
-
-        @pl.when((s >= 1) & (s <= chunks))
-        def _():
-            finish_chunk(s - 1)
-
-        @pl.when(s >= 2)
-        def _():
-            relay_chunk(s - 2)
+                at_step(s - sent(high) - hop * i, lambda c: relay(high, c, has_left, left))
+
+    term_ref[...] = lax.dot_general(
+        acc[z], inner[...], (((0,), (0,)), ((), ())), precision=HIGHEST, preferred_element_type=F32
+    )
 
     @pl.loop(0, chunks)
     def _(c):
@@ -365,14 +426,15 @@
                     pass_on(d, c, right).wait_send()
 
 
-def middle(part, weight, cotangent, n_col):
+def middle(part, weight, cotangent, n_col, chunks=8, skew=1, extra=0, hop=1):
     rows, width = cotangent.shape
-    zs, chunks = n_col // 2, 4
+    zs = n_col // 2
     grid2 = pltpu.SemaphoreType.DMA((zs, chunks))
     vmem = pl.BlockSpec(memory_space=pltpu.VMEM)
-    blocks = pltpu.VMEM((zs, rows, width), F32)
+    blocks, own = pltpu.VMEM((zs, rows, width), F32), pltpu.VMEM((rows, width), F32)
+    half = pltpu.VMEM((width, width), BF16)
     return pl.pallas_call(
-        functools.partial(middle_kernel, zs, chunks),
+        functools.partial(middle_kernel, zs, chunks, skew, extra, hop),
         in_specs=[pl.BlockSpec(memory_space=pl.ANY), vmem, vmem],
         out_specs=(vmem, pl.BlockSpec(memory_space=pl.ANY), vmem),
         out_shape=(
@@ -381,7 +443,7 @@
             jax.ShapeDtypeStruct((width, width), F32),
         ),
         scratch_shapes=[
-            blocks, blocks, blocks, blocks, pltpu.VMEM((rows, width), F32),
+            blocks, blocks, blocks, blocks, own, own, half, half, half, half,
             pltpu.SemaphoreType.DMA((zs,)), grid2, grid2, grid2, grid2, grid2, grid2,
             grid2, pltpu.SemaphoreType.DMA((chunks,)), grid2, grid2, grid2, pltpu.SemaphoreType.DMA((chunks,)),
         ],
@@ -476,7 +538,138 @@
         spread(j, lax.rem(col + n_col - j, n_col)).wait_recv()
 
 
-def last(part, term, n_row, n_col, scale):
+def last_square_kernel(
+    parts, n_col, scale,
+    part_ref, term_ref,
+    out_ref, total_ref,
+    mine, middle_rows, near, through, final, first, second,
+    own_sem, middle_sem, send_sem, recv_sem, send1, recv1, send2, recv2, send3, recv3,
+):
+    row, col = lax.axis_index("row"), lax.axis_index("col")
+    rows = out_ref.shape[0]
+    size, half = rows // parts, parts // 2
+    piece = term_ref.shape[0] // n_col
+    x_bit, y_bit = lax.rem(row, 2), lax.div(row, 2)
+    by_x, by_y, corner = y_bit * 2 + (1 - x_bit), (1 - y_bit) * 2 + x_bit, 3 - row
+    barrier = pltpu.get_barrier_semaphore()
+    for peer in (by_x, by_y, corner):
+        pl.semaphore_signal(barrier, inc=1, device_id={"row": peer}, device_id_type=MESH)
+    for j in range(1, n_col):
+        pl.semaphore_signal(barrier, inc=1, device_id={"col": lax.rem(col + j, n_col)}, device_id_type=MESH)
+    pl.semaphore_wait(barrier, n_col + 2)
+
+    def remote(src, dst, send, recv, device):
+        return pltpu.make_async_remote_copy(
+            src_ref=src, dst_ref=dst, send_sem=send, recv_sem=recv, device_id=device, device_id_type=MESH
+        )
+
+    def span(q):
+        return pl.ds(q * size, size)
+
+    def block(owner, q):
+        return part_ref.at[pl.ds(pl.multiple_of(owner * rows + q * size, size), size), :]
+
+    def rows_of(i):
+        return pl.ds(pl.multiple_of(i * piece, piece), piece)
+
+    def hop(q, second_hop):
+        return {"row": by_x if (q < half) != second_hop else by_y}
+
+    def far(q):
+        return remote(block(corner, q), through.at[span(q), :], send_sem.at[0, q], recv_sem.at[0, q], hop(q, False))
+
+    def direct(q):
+        to = by_x if q < half else by_y
+        return remote(block(to, q), near.at[span(q), :], send_sem.at[1, q], recv_sem.at[1, q], hop(q, False))
+
+    def onward(q):
+        return remote(
+            middle_rows.at[span(q), :], final.at[span(q), :], send_sem.at[2, q], recv_sem.at[2, q], hop(q, True)
+        )
+
+    def load_middle(q):
+        return pltpu.make_async_copy(block(by_y if q < half else by_x, q), middle_rows.at[span(q), :], middle_sem.at[q])
+
+    def scatter(j):
+        to = lax.rem(col + j, n_col)
+        return remote(term_ref.at[rows_of(to), :], first.at[j], send1.at[j], recv1.at[j], {"col": to})
+
+    def exchange(j, slot):
+        return remote(first.at[0], second.at[slot], send2.at[j], recv2.at[j], {"row": lax.rem(row + j, 4)})
+
+    def spread(j, owner):
+        where = total_ref.at[rows_of(owner), :]
+        return remote(where, where, send3.at[j], recv3.at[j], {"col": lax.rem(col + j, n_col)})
+
+    order = [q for pair in zip(range(half), range(half, parts)) for q in pair]
+    for j in range(1, n_col):
+        scatter(j).start()
+    for q in order:
+        far(q).start()
+    own = pltpu.make_async_copy(part_ref.at[pl.ds(pl.multiple_of(row * rows, rows), rows), :], mine, own_sem)
+    own.start()
+    for q in order:
+        load_middle(q).start()
+    first[0] = term_ref[rows_of(col), :]
+    for j in range(1, n_col):
+        scatter(j).wait_recv()
+        first[0] += first[j]
+    for j in range(1, 4):
+        exchange(j, row).start()
+    for q in order:
+        direct(q).start()
+    second[row] = first[0]
+    for q in order:
+        load_middle(q).wait()
+        far(q).wait_recv()
+        middle_rows[span(q), :] += through[span(q), :]
+        onward(q).start()
+    for j in range(1, 4):
+        exchange(j, lax.rem(row + 4 - j, 4)).wait_recv()
+    total_ref[rows_of(col), :] = (second[0] + second[1] + second[2] + second[3]) * scale
+    for j in range(1, n_col):
+        spread(j, col).start()
+    own.wait()
+    for q in order:
+        direct(q).wait_recv()
+        onward(q).wait_recv()
+        out_ref[span(q), :] = mine[span(q), :] + near[span(q), :] + final[span(q), :]
+    for q in order:
+        far(q).wait_send()
+        direct(q).wait_send()
+        onward(q).wait_send()
+    for j in range(1, 4):
+        exchange(j, row).wait_send()
+    for j in range(1, n_col):
+        scatter(j).wait_send()
+        spread(j, col).wait_send()
+        spread(j, lax.rem(col + n_col - j, n_col)).wait_recv()
+
+
+def last_square(part, term, n_col, scale, parts):
+    rows, width = part.shape[0] // 4, part.shape[1]
+    piece = term.shape[0] // n_col
+    vmem, own = pl.BlockSpec(memory_space=pltpu.VMEM), pltpu.VMEM((rows, width), F32)
+    bulk, by_row, by_col = (pltpu.SemaphoreType.DMA(n) for n in ((3, parts), (4,), (n_col,)))
+    return pl.pallas_call(
+        functools.partial(last_square_kernel, parts, n_col, scale),
+        in_specs=[pl.BlockSpec(memory_space=pl.ANY), vmem],
+        out_specs=(vmem, vmem),
+        out_shape=(jax.ShapeDtypeStruct((rows, width), F32), jax.ShapeDtypeStruct(term.shape, F32)),
+        scratch_shapes=[
+            own, own, own, own, own,
+            pltpu.VMEM((n_col, piece, width), F32),
+            pltpu.VMEM((4, piece, width), F32),
+            pltpu.SemaphoreType.DMA, pltpu.SemaphoreType.DMA((parts,)), bulk, bulk,
+            by_col, by_col, by_row, by_row, by_col, by_col,
+        ],
+        compiler_params=params(2),
+    )(part, term)
+
+
+def last(part, term, n_row, n_col, scale, parts=4):
+    if n_row == 4:
+        return last_square(part, term, n_col, scale, parts)
     rows, width = part.shape[0] // n_row, part.shape[1]
     piece = term.shape[0] // n_col
     vmem = pl.BlockSpec(memory_space=pltpu.VMEM)

time: 185 us -> 149 us (0.81)
  Pallas kernels: 177 us -> 141 us
    pallas_call x3, Pallas kernels: 163 us -> 123 us  [the longest x1 72.5 us: middle(): pl.pallas_call(functools.partial(middle_kernel, zs, chunks, skew, extra,...]
    pallas_call x2, Pallas kernels: 14.1 us -> 18.1 us  [combine_tiles(): pl.pallas_call(functools.partial(tile_kernel, group, transpose), grid_spe...]
where the time goes in v1:
time: 149 us; the launch traced here: 147 us
  Pallas kernels  141 us (95%)
  local copies, waits for them, and re-layouts  4.34 us (3%)
    pallas_call x1, Pallas kernels, middle(): pl.pallas_call(functools.partial(middle_kernel, zs, chunks, skew, extra,...  72.5 us
    pallas_call x1, Pallas kernels, last_square(): pl.pallas_call(functools.partial(last_square_kernel, parts, n_col, scale)...  27.8 us
    pallas_call x1, Pallas kernels, gather_rows(): pl.pallas_call(functools.partial(gather_square_kernel, parts) if square e...  22.5 us
    pallas_call x2, Pallas kernels, combine_tiles(): pl.pallas_call(functools.partial(tile_kernel, group, transpose), grid_spe...  18.1 us
    unnamed x5, local copies, waits for them, and re-layouts  4.34 us

profile of v1, /device:TPU:0, one launch (start us, length us, event | category | flops | bytes accessed | tf_op | source)
XLA Modules:
  0.0 146.6 jit_solution(17652733552911986096)
XLA Ops:
  1.3 22.5 %shard_map.94.source_ref = f32[2048,256]{1,0:T(8,128)} custom-call(f32[512,256]{1,0:T(8,128)} %x_ref.1), custom_call_target="tpu_custom_call" | custom-call | tf_op jit(solution)/shard_map/pallas_call | solution.py:185
  23.8 8.8 %shard_map.95.part_ref = f32[4096,256]{1,0:T(8,128)} custom-call(s32[128]{0:T(128)} %bitcast.8, s32[128]{0:T(128)} %bitcast.10, s32[1]{0:T(128)} %bitcast.4.count_ref, f32[128,128,128]{2,1,0:T(8,128)} %bitcast.6, f32[2048,256]{1,0:T(8,128)} %shard_map.94.source_ref), custom_call_target="tpu_custom_call" | custom-call | tf_op jit(solution)/shard_map/pallas_call | solution.py:80
  32.6 72.5 %shard_map.96 = (f32[512,256]{1,0:T(8,128)}, f32[4096,256]{1,0:T(8,128)}, f32[256,256]{1,0:T(8,128)}) custom-call(f32[4096,256]{1,0:T(8,128)} %shard_map.95.part_ref, f32[256,256]{1,0:T(8,128)} %weight_ref.1, f32[512,256]{1,0:T(8,128)} %cot_ref.1), custom_call_target="tpu_custom_call" | custom-call | tf_op jit(solution)/shard_map/pallas_call | solution.py:436
  105.1 0.0 copy-start
  105.1 9.3 %shard_map.97.part_ref = f32[2048,256]{1,0:T(8,128)} custom-call(s32[128]{0:T(128)} %bitcast.11, s32[128]{0:T(128)} %bitcast.9, s32[1]{0:T(128)} %bitcast.5.count_ref, f32[128,128,128]{2,1,0:T(8,128)} %bitcast.7, f32[4096,256]{1,0:T(8,128)} %get-tuple-element.9.source_ref), custom_call_target="tpu_custom_call" | custom-call | tf_op jit(solution)/shard_map/pallas_call | solution.py:80
  114.4 27.8 %shard_map.98 = (f32[512,256]{1,0:T(8,128)}, f32[256,256]{1,0:T(8,128)}) custom-call(f32[2048,256]{1,0:T(8,128)} %shard_map.97.part_ref, f32[256,256]{1,0:T(8,128)} %get-tuple-element.10.term_ref), custom_call_target="tpu_custom_call" | custom-call | tf_op jit(solution)/shard_map/pallas_call | solution.py:654
  142.2 0.0 copy-done
  142.3 0.8 copy.14
  143.1 1.9 %copy.15 = f32[512,256]{1,0:T(8,128)} copy(f32[512,256]{1,0:T(8,128)} %get-tuple-element.17) | data formatting | bytes 1048576
  144.9 1.7 %copy.16 = f32[256,256]{1,0:T(8,128)} copy(f32[256,256]{1,0:T(8,128)} %get-tuple-element.18) | data formatting | bytes 524288
Async XLA Ops:
  105.1 37.1 %copy-start = (f32[512,256]{1,0:T(8,128)S(1)}, f32[512,256]{1,0:T(8,128)}, u32[]{:S(2)}) copy-start(f32[512,256]{1,0:T(8,128)} %get-tuple-element.16) | copy-start | bytes 1572868

commit v2 on v1

--- a/solution.py
+++ b/solution.py
@@ -12,7 +12,6 @@
 BF16 = jnp.bfloat16
 MESH = pl.DeviceIdType.MESH
 VMEM_LIMIT = 60 * 1024 * 1024
-DENSE = True
 HIGHEST = lax.Precision.HIGHEST
 
 
@@ -35,13 +34,16 @@
     )
 
 
-def tile_kernel(group, transpose, fetch_ref, put_ref, count_ref, tiles_ref, source_ref, out_ref, hi_ref, lo_ref):
+def tile_kernel(group, transpose, fetch_ref, put_ref, count_ref, tiles_ref, source_ref, *refs):
+    *carry, out_ref, hi_ref, lo_ref = refs
     step = pl.program_id(0)
     edge = tiles_ref.shape[1]
 
     @pl.when(step == 0)
     def _():
         out_ref[...] = jnp.zeros_like(out_ref)
+        if carry:
+            carry[1][...] = carry[0][...]
 
         @pl.loop(0, source_ref.shape[0] // edge)
         def _(b):
@@ -69,13 +71,16 @@
             out_ref[put, :] += product
 
 
-def combine_tiles(tiles, fetch_ids, put_ids, count, source, out_rows, transpose):
+def combine_tiles(tiles, fetch_ids, put_ids, count, source, out_rows, transpose, carry=()):
     slots, edge, _ = tiles.shape
     width = source.shape[1]
     group = math.gcd(16, slots)
 
     def tile_index(i, fetch, put, n):
         return (jnp.minimum(i, (n[0] - 1) // group), 0, 0)
+
+    def whole(shape):
+        return pl.BlockSpec(shape, lambda i, *_: (0, 0), pipeline_mode=pl.Buffered(1))
 
     return pl.pallas_call(
         functools.partial(tile_kernel, group, transpose),
@@ -84,14 +89,18 @@
             grid=(slots // group,),
             in_specs=[
                 pl.BlockSpec((group, edge, edge), tile_index),
-                pl.BlockSpec(source.shape, lambda i, *_: (0, 0), pipeline_mode=pl.Buffered(1)),
+                whole(source.shape),
+                *(whole(x.shape) for x in carry),
             ],
-            out_specs=pl.BlockSpec((out_rows, width), lambda i, *_: (0, 0), pipeline_mode=pl.Buffered(1)),
+            out_specs=(*(whole(x.shape) for x in carry), whole((out_rows, width))),
             scratch_shapes=[pltpu.VMEM(source.shape, BF16), pltpu.VMEM(source.shape, BF16)],
         ),
-        out_shape=jax.ShapeDtypeStruct((out_rows, width), F32),
+        out_shape=(
+            *(jax.ShapeDtypeStruct(x.shape, F32) for x in carry),
+            jax.ShapeDtypeStruct((out_rows, width), F32),
+        ),
         compiler_params=params(),
-    )(fetch_ids, put_ids, count, tiles, source)
+    )(fetch_ids, put_ids, count, tiles, source, *carry)
 
 
 def gather_kernel(n, x_ref, out_ref, send_sem, recv_sem, own_sem):
@@ -179,7 +188,7 @@
         onward(q).wait_send()
 
 
-def gather_rows(x, n, parts=8):
+def gather_rows(x, n, parts=4):
     square = n == 4
     shape = (3, parts) if square else (n,)
     return pl.pallas_call(
@@ -327,7 +336,7 @@
             to_left(z, c).wait_recv()
             acc[z, span(c)] += from_right[z, span(c)]
 
-        if DENSE:
+        if True:
             summed = acc[z, span(c)]
             pre = dot3(summed, w_hi[...], w_lo[...])
             sigma = jax.nn.sigmoid(pre)
@@ -610,14 +619,14 @@
     own.start()
     for q in order:
         load_middle(q).start()
+    for q in order:
+        direct(q).start()
     first[0] = term_ref[rows_of(col), :]
     for j in range(1, n_col):
         scatter(j).wait_recv()
         first[0] += first[j]
     for j in range(1, 4):
         exchange(j, row).start()
-    for q in order:
-        direct(q).start()
     second[row] = first[0]
     for q in order:
         load_middle(q).wait()
@@ -694,9 +703,9 @@
     count = tile_count.reshape(1)
     rows = features.shape[0]
     gathered = gather_rows(features, n_row)
-    part = combine_tiles(tiles, col_ids, row_ids, count, gathered, rows * n_col, False)
+    (part,) = combine_tiles(tiles, col_ids, row_ids, count, gathered, rows * n_col, False)
     output, grads, term = middle(part, weight, cotangent, n_col)
-    part_grad = combine_tiles(tiles, row_ids, col_ids, count, grads, rows * n_row, True)
+    output, part_grad = combine_tiles(tiles, row_ids, col_ids, count, grads, rows * n_row, True, (output,))
     scale = 1.0 / math.sqrt(rows * n_row * n_col)
     returned, weight_grad = last(part_grad, term, n_row, n_col, scale)
     return (output, returned, weight_grad)

time: 149 us -> 149 us (level); the launches traced: 147 us -> 149 us
  Pallas kernels: 141 us -> 144 us
    pallas_call x1, Pallas kernels: 27.8 us -> 29.8 us  [last_square(): pl.pallas_call(functools.partial(last_square_kernel, parts, n_col, scale)...]
    unnamed x5 -> x2, local copies, waits for them, and re-layouts: 4.34 us -> 3.54 us
where the time goes in v2:
time: 149 us
  Pallas kernels  144 us (97%)
  local copies, waits for them, and re-layouts  3.54 us (2%)
    pallas_call x1, Pallas kernels, middle(): pl.pallas_call(functools.partial(middle_kernel, zs, chunks, skew, extra,...  73.5 us
    pallas_call x1, Pallas kernels, last_square(): pl.pallas_call(functools.partial(last_square_kernel, parts, n_col, scale)...  29.8 us
    pallas_call x1, Pallas kernels, gather_rows(): pl.pallas_call(functools.partial(gather_square_kernel, parts) if square e...  22.3 us
    pallas_call x2, Pallas kernels, combine_tiles(): pl.pallas_call(functools.partial(tile_kernel, group, transpose), grid_spe...  18.2 us
    unnamed x2, local copies, waits for them, and re-layouts  3.54 us

profile of v2, /device:TPU:0, one launch (start us, length us, event | category | flops | bytes accessed | tf_op | source)
XLA Modules:
  0.0 148.7 jit_solution(4053771871290500854)
XLA Ops:
  1.3 22.3 %shard_map.94.source_ref = f32[2048,256]{1,0:T(8,128)} custom-call(f32[512,256]{1,0:T(8,128)} %x_ref.1), custom_call_target="tpu_custom_call" | custom-call | tf_op jit(solution)/shard_map/pallas_call | solution.py:194
  23.6 8.8 %shard_map.95.part_ref = f32[4096,256]{1,0:T(8,128)} custom-call(s32[128]{0:T(128)} %bitcast.10, s32[128]{0:T(128)} %bitcast.8, s32[1]{0:T(128)} %bitcast.4.count_ref, f32[128,128,128]{2,1,0:T(8,128)} %bitcast.6, f32[2048,256]{1,0:T(8,128)} %shard_map.94.source_ref), custom_call_target="tpu_custom_call" | custom-call | tf_op jit(solution)/shard_map/pallas_call | solution.py:85
  32.4 73.5 %shard_map.96 = (f32[512,256]{1,0:T(8,128)}, f32[4096,256]{1,0:T(8,128)}, f32[256,256]{1,0:T(8,128)}) custom-call(f32[4096,256]{1,0:T(8,128)} %shard_map.95.part_ref, f32[256,256]{1,0:T(8,128)} %weight_ref.1, f32[512,256]{1,0:T(8,128)} %cot_ref.1), custom_call_target="tpu_custom_call" | custom-call | tf_op jit(solution)/shard_map/pallas_call | solution.py:445
  105.9 9.5 %shard_map.97 = (f32[512,256]{1,0:T(8,128)}, f32[2048,256]{1,0:T(8,128)}) custom-call(s32[128]{0:T(128)} %bitcast.9, s32[128]{0:T(128)} %bitcast.11, s32[1]{0:T(128)} %bitcast.5.count_ref, f32[128,128,128]{2,1,0:T(8,128)} %bitcast.7, f32[4096,256]{1,0:T(8,128)} %get-tuple-element.10.source_ref, f32[512,256]{1,0:T(8,128)} %get-tuple-element.11.refs_0_), custom_call_target="tpu_custom_call" | custom-call | tf_op jit(solution)/shard_map/pallas_call | solution.py:85
  115.4 29.8 %shard_map.98 = (f32[512,256]{1,0:T(8,128)}, f32[256,256]{1,0:T(8,128)}) custom-call(f32[2048,256]{1,0:T(8,128)} %get-tuple-element.13.part_ref, f32[256,256]{1,0:T(8,128)} %get-tuple-element.14.term_ref), custom_call_target="tpu_custom_call" | custom-call | tf_op jit(solution)/shard_map/pallas_call | solution.py:663
  145.2 1.9 %copy.13 = f32[512,256]{1,0:T(8,128)} copy(f32[512,256]{1,0:T(8,128)} %get-tuple-element.21) | data formatting | bytes 1048576
  147.1 1.7 %copy.14 = f32[256,256]{1,0:T(8,128)} copy(f32[256,256]{1,0:T(8,128)} %get-tuple-element.22) | data formatting | bytes 524288
